TPU v7x, 1024 devices: a whole 4x8x16 slice. The times are simulated.
1024 devices in a mesh: clip: 16 (over y, core), seq: 16 (over z), help: 4 (over x).
Axes of the slice: x: 4, y: 8, z: 16, core: 2. Of those that a mesh axis runs over, the one named last changes fastest.
Arguments:
- query_states: bfloat16 [131072, 2048], P(('clip', 'seq', 'help')), parts along dimension 0, may hold values from -8 to 8
- key_states: bfloat16 [131072, 2048], P(('clip', 'seq', 'help')), parts along dimension 0, may hold values from -8 to 8
- value_states: bfloat16 [131072, 2048], P(('clip', 'seq', 'help')), parts along dimension 0, may hold values from -6 to 6
- tile_lists: int32 [256, 64, 16], P('clip'), parts along dimension 0, may hold values from 0 to 63, as said below
- tile_counts: int32 [256, 64], P('clip'), parts along dimension 0, may hold values from 1 to 16, as said below
Outputs:
- attended: bfloat16 [131072, 2048], P(('clip', 'seq', 'help')), parts along dimension 0
There are 16 independent parts, one for each index of `clip`. A program takes and returns all parts, laid end to end along the dimension named above; each array names one. Nothing has to cross between parts.
Inputs may be any that keep to these rules, and one draw needn't show every extreme that they name: tile_lists[h, t, :] holds 16 different key tiles, the first of which is t itself; the entries at slots tile_counts[h, t] and beyond are ignored. `tile_counts`: in every head some query tile has count 16.
All inputs are finite; a program needn't handle non-finite values.
Results may differ from a plain program's by a relative error of at most 0.0044.
Values may be sent and summed in bfloat16 or wider, within the bound.
A program may use at most 32 MiB of HBM per device.

v0:
```python
import jax
import jax.numpy as jnp
from jax import lax
from jax.sharding import PartitionSpec as P

H = 16
DH = 128
TILE = 128
ROUND = 4


big_negative = -1e30


def pick_tiles(table, index):
    table_rows = table.shape[0]
    selector = (index[:, None] == jnp.arange(table_rows, dtype=jnp.int32)[None, :]).astype(
        jnp.bfloat16
    )
    picked = jnp.dot(selector, table.reshape(table_rows, -1), preferred_element_type=jnp.float32)
    return picked.astype(jnp.bfloat16).reshape((index.shape[0],) + table.shape[1:])


def attend_items(query_items, key_tiles, value_tiles, item_lists, item_counts):
    item_total, tile_rows, head_width = query_items.shape
    factor = head_width ** (-0.5)
    batches = item_total // ROUND
    joined = jnp.concatenate((key_tiles, value_tiles), axis=2)

    def one_batch(packed):
        queries, lists, counts = packed
        start_state = (
            jnp.full((ROUND, tile_rows, 1), big_negative, jnp.float32),
            jnp.zeros((ROUND, tile_rows, 1), jnp.float32),
            jnp.zeros((ROUND, tile_rows, head_width), jnp.float32),
        )

        def one_slot(slot_index, carried):
            running_max, running_sum, weighted = carried
            chosen = lax.dynamic_index_in_dim(lists, slot_index, axis=1, keepdims=False)
            both_blocks = pick_tiles(joined, chosen)
            key_block = both_blocks[:, :, :head_width]
            value_block = both_blocks[:, :, head_width:]
            scores = (
                jnp.einsum("qtd,qsd->qts", queries, key_block, preferred_element_type=jnp.float32)
                * factor
            )
            new_max = jnp.maximum(running_max, jnp.max(scores, axis=2, keepdims=True))
            shrink = jnp.exp(running_max - new_max)
            tile_weights = jnp.exp(scores - new_max)
            new_sum = running_sum * shrink + jnp.sum(tile_weights, axis=2, keepdims=True)
            new_weighted = weighted * shrink + jnp.einsum(
                "qts,qsd->qtd",
                tile_weights.astype(jnp.bfloat16),
                value_block,
                preferred_element_type=jnp.float32,
            )
            live = (slot_index < counts)[:, None, None]
            return (
                jnp.where(live, new_max, running_max),
                jnp.where(live, new_sum, running_sum),
                jnp.where(live, new_weighted, weighted),
            )

        final_state = lax.fori_loop(0, jnp.max(counts), one_slot, start_state)
        return (final_state[2] / final_state[1]).astype(jnp.bfloat16)

    finished = lax.map(
        one_batch,
        (
            query_items.reshape(batches, ROUND, tile_rows, head_width),
            item_lists.reshape(batches, ROUND, item_lists.shape[1]),
            item_counts.reshape(batches, ROUND),
        ),
    )
    return finished.reshape(item_total, tile_rows, head_width)


def shards(query_states, key_states, value_states, tile_lists, tile_counts):
    groups = lax.axis_size("seq")
    helpers = lax.axis_size("help")
    device = lax.axis_index("seq")
    helper = lax.axis_index("help")
    row_count = query_states.shape[0]
    heads_here = H // groups
    head_cols = heads_here * DH
    tile_total = tile_lists.shape[1]
    per_block = row_count // TILE
    owned_total = groups * per_block

    def to_groups(states):
        return states.reshape(row_count, groups, head_cols)

    arrived = (
        lax.all_to_all(to_groups(query_states), "seq", split_axis=1, concat_axis=0, tiled=True),
        lax.all_to_all(to_groups(key_states), "seq", split_axis=1, concat_axis=0, tiled=True),
        lax.all_to_all(to_groups(value_states), "seq", split_axis=1, concat_axis=0, tiled=True),
    )
    arrived_query = arrived[0].reshape(groups, 1, row_count, head_cols)
    arrived_key = arrived[1].reshape(groups, 1, row_count, head_cols)
    arrived_value = arrived[2].reshape(groups, 1, row_count, head_cols)
    head_lists = lax.dynamic_slice_in_dim(tile_lists, device * heads_here, heads_here, 0)
    head_counts = lax.dynamic_slice_in_dim(tile_counts, device * heads_here, heads_here, 0)
    head_offset = (jnp.arange(heads_here, dtype=jnp.int32) * tile_total)[:, None, None]
    flat_lists = (head_lists + head_offset).reshape(heads_here * tile_total, head_lists.shape[2])
    flat_counts = head_counts.reshape(heads_here * tile_total)

    def head_tiles(whole):
        shaped = whole.reshape(tile_total, TILE, heads_here, DH).transpose(2, 0, 1, 3)
        return shaped.reshape(heads_here * tile_total, TILE, DH)

    key_whole, value_whole = (
        lax.all_gather(arrived_key, "help", axis=1, tiled=True),
        lax.all_gather(arrived_value, "help", axis=1, tiled=True),
    )
    key_tiles = head_tiles(key_whole)
    value_tiles = head_tiles(value_whole)
    own_tiles = arrived_query.reshape(owned_total, TILE, heads_here, DH).transpose(2, 0, 1, 3)
    own_tiles = own_tiles.reshape(heads_here * owned_total, TILE, DH)
    local_index = jnp.arange(owned_total, dtype=jnp.int32)
    global_tile = (
        local_index // per_block * helpers + helper
    ) * per_block + local_index % per_block
    item_index = (
        jnp.arange(heads_here, dtype=jnp.int32)[:, None] * tile_total + global_tile[None, :]
    )
    item_index = item_index.reshape(heads_here * owned_total)
    results = attend_items(
        own_tiles,
        key_tiles,
        value_tiles,
        jnp.take(flat_lists, item_index, axis=0),
        jnp.take(flat_counts, item_index, axis=0),
    )
    owned = results.reshape(heads_here, owned_total, TILE, DH)
    leaving = owned.transpose(1, 2, 0, 3)
    leaving = leaving.reshape(groups, row_count, head_cols)
    returned = lax.all_to_all(leaving, "seq", split_axis=0, concat_axis=2, tiled=True)
    return returned.reshape(row_count, H * DH)


def solution(mesh):
    placed = (
        P(("clip", "seq", "help"), None),
        P(("clip", "seq", "help"), None),
        P(("clip", "seq", "help"), None),
        P("clip", None, None),
        P("clip", None),
    )
    return jax.shard_map(
        shards,
        mesh=mesh,
        in_specs=placed,
        out_specs=P(("clip", "seq", "help"), None),
        check_vma=False,
    )
```

profile of v0, /device:TPU:81, one launch (start us, length us, event | category | flops | bytes accessed | tf_op | source)
XLA Modules:
  0.0 606.9 jit_solution(5510492906560778502)
XLA Ops:
  6.5 1.0 copy-done
  7.7 42.5 %all_to_all.60 = bf16[128,16,128]{2,0,1:T(8,128)(2,1)} all-to-all(bf16[128,16,128]{2,0,1:T(8,128)(2,1)S(1)} %copy_bitcast_fusion.2), channel_id=1, replica_groups=mesh['clip'=16,'seq'=16,'help'=4] {'seq'}, dimensions={1} | all-to-all | bytes 1048576 | tf_op jit(solution)/shard_map/all_to_all | solution.py:96
  50.3 1.2 copy_bitcast_fusion.1
  51.5 35.3 %all_to_all.61 = bf16[128,16,128]{2,0,1:T(8,128)(2,1)} all-to-all(bf16[128,16,128]{2,0,1:T(8,128)(2,1)S(1)} %copy_bitcast_fusion.1), channel_id=1, replica_groups=mesh['clip'=16,'seq'=16,'help'=4] {'seq'}, dimensions={1} | all-to-all | bytes 1048576 | tf_op jit(solution)/shard_map/all_to_all | solution.py:97
  86.9 0.9 copy_bitcast_fusion.3
  87.8 10.6 %all-to-all-start = ((bf16[128,16,128]{2,0,1:T(8,128)(2,1)}), bf16[128,16,128]{2,0,1:T(8,128)(2,1)S(1)}, u32[]{:S(2)}, u32[]{:S(2)}) async-start(bf16[128,16,128]{2,0,1:T(8,128)(2,1)} %copy_bitcast_fusion.3), calls=%async_computation | async-start | bytes 1048576 | tf_op jit(solution)/shard_map/all_to_all | solution.py:95
  98.5 0.7 constant_dynamic-slice_fusion.1
  99.8 0.7 dynamic-slice_bitcast_fusion.3
  100.5 0.7 gather_fusion
  101.4 34.6 %all-gather.7.cloned.1.call-done = bf16[16,512,1,128]{3,1,0,2:T(8,128)(2,1)} async-done(((bf16[16,128,1,128]{3,1,0,2:T(8,128)(2,1)}), bf16[16,512,1,128]{3,1,0,2:T(8,128)(2,1)}) %all-gather.7.cloned.1.call-update) | async-done | bytes 2097168 | tf_op jit(solution)/shard_map/all_gather | solution.py:114
  136.0 4.9 pad_maximum_fusion
  140.9 157.2 %while.25 = (s32[]{:T(128)}, bf16[4,4,128,128]{3,2,1,0:T(8,128)(2,1)S(1)}, s32[4,4]{1,0:T(4,128)S(1)}, s32[4,4,16]{2,1,0:T(4,128)S(1)}, bf16[4,4,128,128]{3,2,1,...) while((s32[]{:T(128)}, ...), condition=%wide.region_6.7_spmd, body=%wide.region_0.6_spmd.sunk | while | flops 51186444 | bytes 16029708 | solution.py:68
  141.7 28.0 %while.26 = (s32[]{:T(128)}, f32[4,128,1]{1,0,2:T(4,128)S(1)}, f32[4,128,1]{1,0,2:T(4,128)S(1)}, f32[4,128,128]{2,1,0:T(8,128)S(1)}, s32[]{:T(128)}, /*index=5*/...) while((s32[]{:T(128)}, f32[4,128,1]{1,0,2:T(4,128)S(1)}, ...), condition=%wide.region_5.5_spmd, body=%wide.region_2.4_spmd.sunk | while | flops 51055368 | bytes 15104743 | solution.py:65
  142.3 4.7 copy.49
  147.1 0.7 convolution_convert_fusion.2
  149.2 4.7 copy.49
  153.9 0.7 convolution_convert_fusion.2
  156.0 4.7 copy.49
  160.8 0.7 convolution_convert_fusion.2
  162.9 4.7 copy.49
  167.6 0.7 convolution_convert_fusion.2
  169.9 0.6 fusion.32
  170.7 69.2 %while.26 = (s32[]{:T(128)}, f32[4,128,1]{1,0,2:T(4,128)S(1)}, f32[4,128,1]{1,0,2:T(4,128)S(1)}, f32[4,128,128]{2,1,0:T(8,128)S(1)}, s32[]{:T(128)}, /*index=5*/...) while((s32[]{:T(128)}, f32[4,128,1]{1,0,2:T(4,128)S(1)}, ...), condition=%wide.region_5.5_spmd, body=%wide.region_2.4_spmd.sunk | while | flops 51055368 | bytes 15104743 | solution.py:65
  171.4 4.7 copy.49
  176.1 0.7 convolution_convert_fusion.2
  178.2 4.7 copy.49
  183.0 0.7 convolution_convert_fusion.2
  185.1 4.7 copy.49
  189.8 0.7 convolution_convert_fusion.2
  191.9 4.7 copy.49
  196.7 0.7 convolution_convert_fusion.2
  198.8 4.7 copy.49
  203.5 0.7 convolution_convert_fusion.2
  205.6 4.7 copy.49
  210.4 0.7 convolution_convert_fusion.2
  212.5 4.7 copy.49
  217.2 0.7 convolution_convert_fusion.2
  219.3 4.7 copy.49
  224.1 0.7 convolution_convert_fusion.2
  226.2 4.7 copy.49
  230.9 0.7 convolution_convert_fusion.2
  233.0 4.7 copy.49
  237.8 0.7 convolution_convert_fusion.2
  240.1 0.6 fusion.32
  240.9 34.9 %while.26 = (s32[]{:T(128)}, f32[4,128,1]{1,0,2:T(4,128)S(1)}, f32[4,128,1]{1,0,2:T(4,128)S(1)}, f32[4,128,128]{2,1,0:T(8,128)S(1)}, s32[]{:T(128)}, /*index=5*/...) while((s32[]{:T(128)}, f32[4,128,1]{1,0,2:T(4,128)S(1)}, ...), condition=%wide.region_5.5_spmd, body=%wide.region_2.4_spmd.sunk | while | flops 51055368 | bytes 15104743 | solution.py:65
  241.5 4.7 copy.49
  246.3 0.7 convolution_convert_fusion.2
  248.4 4.7 copy.49
  253.1 0.7 convolution_convert_fusion.2
  255.2 4.7 copy.49
  260.0 0.7 convolution_convert_fusion.2
  262.1 4.7 copy.49
  266.8 0.7 convolution_convert_fusion.2
  268.9 4.7 copy.49
  273.7 0.7 convolution_convert_fusion.2
  276.7 21.2 %while.26 = (s32[]{:T(128)}, f32[4,128,1]{1,0,2:T(4,128)S(1)}, f32[4,128,1]{1,0,2:T(4,128)S(1)}, f32[4,128,128]{2,1,0:T(8,128)S(1)}, s32[]{:T(128)}, /*index=5*/...) while((s32[]{:T(128)}, f32[4,128,1]{1,0,2:T(4,128)S(1)}, ...), condition=%wide.region_5.5_spmd, body=%wide.region_2.4_spmd.sunk | while | flops 51055368 | bytes 15104743 | solution.py:65
  277.4 4.7 copy.49
  282.1 0.7 convolution_convert_fusion.2
  284.2 4.7 copy.49
  289.0 0.7 convolution_convert_fusion.2
  291.1 4.7 copy.49
  295.8 0.7 convolution_convert_fusion.2
  298.1 300.6 %all_to_all.62 = bf16[16,128,128]{2,1,0:T(8,128)(2,1)S(1)} all-to-all(bf16[16,128,128]{2,1,0:T(8,128)(2,1)S(1)} %bitcast.125), channel_id=1, replica_groups=mesh['clip'=16,'seq'=16,'help'=4] {'seq'}, dimensions={0} | all-to-all | bytes 1048576 | tf_op jit(solution)/shard_map/all_to_all | solution.py:138
  599.0 1.0 copy.33
  (226 shorter events, 19.6 us)
Async XLA Ops:
  6.5 1.0 copy-start
  6.5 80.3 %copy-start.1 = (bf16[128,2048]{1,0:T(8,128)(2,1)S(1)}, bf16[128,2048]{1,0:T(8,128)(2,1)}, u32[]{:S(2)}) copy-start(bf16[128,2048]{1,0:T(8,128)(2,1)} %param.9) | copy-start | bytes 1572868
  6.5 94.8 %all-gather.5.cloned.1.call-start = ((), (), s32[]{:S(2)}) async-start(), calls=%async_computation.4 | async-start | bytes 2621440 | tf_op jit(solution)/shard_map/all_gather | solution.py:113
  50.3 85.8 %all-gather.7.cloned.1.call-start = ((), (), s32[]{:S(2)}) async-start(), calls=%async_computation.5 | async-start | bytes 2621440 | tf_op jit(solution)/shard_map/all_gather | solution.py:114
  87.8 53.1 %all-to-all-start = ((bf16[128,16,128]{2,0,1:T(8,128)(2,1)}), bf16[128,16,128]{2,0,1:T(8,128)(2,1)S(1)}, u32[]{:S(2)}, u32[]{:S(2)}) async-start(bf16[128,16,128]{2,0,1:T(8,128)(2,1)} %copy_bitcast_fusion.3), calls=%async_computation | async-start | bytes 1048576 | tf_op jit(solution)/shard_map/all_to_all | solution.py:95
Sparse Core Ops, SparseCore 0:
  50.4 41.0 all-gather.4
  94.2 41.7 all-gather.6
where the time goes:
time: 610 us; the launch traced here: 607 us
  blocking collectives  378 us (62%)
  local copies, waits for them, and re-layouts  113 us (19%)
  waiting for transfers between devices  34.7 us (6%)
  matrix products  27.4 us (4%)
  loops' own time  17.5 us (3%)
  between operations  13.5 us (2%)
  other arithmetic  11.5 us (2%)
  starting transfers between devices  10.7 us (2%)
    all_to_all x1, blocking collectives, shards(): lax.all_to_all(leaving, 'seq', split_axis=0, concat_axis=2, tiled=True)  301 us
    while x44, local copies, waits for them, and re-layouts  105 us
    all_to_all x1, blocking collectives, shards(): lax.all_to_all(to_groups(key_states), 'seq', split_axis=1, concat_axis=0,...  42.5 us
    all_to_all x1, blocking collectives, shards(): lax.all_to_all(to_groups(value_states), 'seq', split_axis=1, concat_axis=...  35.3 us
    all_gather x1, waiting for transfers between devices, shards(): lax.all_gather(arrived_value, 'help', axis=1, tiled=True)  34.6 us
    another operation x4, loops' own time, one_batch(): final_state = lax.fori_loop(0, jnp.max(counts), one_slot, start_state)  17.2 us
    dot_general x22, matrix products, pick_tiles(): jnp.dot(selector, table.reshape(table_rows, -1), preferred_element_type=j...  15.7 us
  transfers between devices with their start and end apart: 3, of which 1 were waited for; matrix products, arithmetic and copies ran while one was open for 2% of the time, Pallas kernels for 0%

commit v1 on v0

v1 whole, which is shorter than its diff:
```python
import functools
import math

import jax
import jax.numpy as jnp
from jax import lax
from jax.experimental import pallas as pl
from jax.experimental.pallas import tpu as pltpu
from jax.sharding import PartitionSpec as P

MESH = pl.DeviceIdType.MESH
TILE = 128
DH = 128
SLOTS = 16


def spread(n, i):
    half = (i + 1) // 2
    return (half * (2 * (i % 2) - 1) + n) % n


def kernel(
    groups, helpers,
    lists_hbm, counts_hbm, q_hbm, k_hbm, v_hbm, out_hbm,
    kv, qs, outs, scores, landed, lists, counts,
    plan_sem, own_sem, send_q, send_kv, send_o, send_x,
    recv_q, recv_kv, recv_o, recv_x, recv_far, write_sem,
):
    z = lax.axis_index("seq")
    x = lax.axis_index("help")
    right = (x + 1) % helpers
    left = (x + helpers - 1) % helpers
    across = (x + 2) % helpers
    mine = z * helpers + x

    plan = [
        pltpu.make_async_copy(lists_hbm.at[z], lists, plan_sem.at[0]),
        pltpu.make_async_copy(counts_hbm, counts, plan_sem.at[1]),
    ]
    for copy in plan:
        copy.start()

    def columns(head):
        return pl.ds(pl.multiple_of(head * DH, DH), DH)

    own = [
        pltpu.make_async_copy(k_hbm.at[:, columns(z)], kv.at[mine, 0], recv_kv.at[z]),
        pltpu.make_async_copy(v_hbm.at[:, columns(z)], kv.at[mine, 1], recv_kv.at[z]),
        pltpu.make_async_copy(q_hbm.at[:, columns(z)], qs.at[z], recv_q.at[z]),
    ]
    for copy in own:
        copy.start()

    barrier = pltpu.get_barrier_semaphore()

    def greet(i, carry):
        pl.semaphore_signal(
            barrier, inc=1, device_id={"seq": (z + i) % groups}, device_id_type=MESH
        )
        return carry

    lax.fori_loop(1, groups, greet, 0)
    for near in (left, right):
        pl.semaphore_signal(barrier, inc=1, device_id={"help": near}, device_id_type=MESH)
    pl.semaphore_wait(barrier, groups + 1)

    def send_keys(i, carry):
        there = (z + spread(groups, i)) % groups
        for which, source in ((0, k_hbm), (1, v_hbm)):
            pltpu.make_async_remote_copy(
                src_ref=source.at[:, columns(there)],
                dst_ref=kv.at[mine, which],
                send_sem=send_kv.at[which],
                recv_sem=recv_kv.at[z],
                device_id={"seq": there},
                device_id_type=MESH,
            ).start()
        return carry

    def send_queries(i, carry):
        there = (z + spread(groups, i)) % groups
        pltpu.make_async_remote_copy(
            src_ref=q_hbm.at[:, columns(there)],
            dst_ref=qs.at[z],
            send_sem=send_q,
            recv_sem=recv_q.at[z],
            device_id={"seq": there},
            device_id_type=MESH,
        ).start()
        return carry

    lax.fori_loop(1, groups, send_keys, 0)
    lax.fori_loop(1, groups, send_queries, 0)

    def tile_copy(tile, way, sem, send, near):
        return pltpu.make_async_remote_copy(
            src_ref=kv.at[tile],
            dst_ref=kv.at[tile],
            send_sem=send_x.at[send],
            recv_sem=sem,
            device_id={"help": near},
            device_id_type=MESH,
        )

    def arrived(ref, sem):
        pltpu.make_async_copy(ref, ref, sem).wait()

    def pass_on(i, carry):
        source = (z + spread(groups, i)) % groups
        tile = source * helpers + x
        arrived(kv.at[tile], recv_kv.at[source])
        tile_copy(tile, 0, recv_x.at[0, source], 0, right).start()
        tile_copy(tile, 1, recv_x.at[1, source], 1, left).start()
        return carry

    def pass_far(i, carry):
        even = (z + spread(groups, i)) % groups
        odd = (z + spread(groups, i + 1)) % groups
        from_left = even * helpers + left
        from_right = odd * helpers + right
        arrived(kv.at[from_left], recv_x.at[0, even])
        tile_copy(from_left, 0, recv_far.at[even], 2, right).start()
        arrived(kv.at[from_right], recv_x.at[1, odd])
        tile_copy(from_right, 1, recv_far.at[odd], 2, left).start()
        return carry

    lax.fori_loop(0, groups, pass_on, 0)
    lax.fori_loop(0, groups // 2, lambda i, c: pass_far(2 * i, c), 0)

    def rest(i, carry):
        even = (z + spread(groups, 2 * i)) % groups
        odd = (z + spread(groups, 2 * i + 1)) % groups
        arrived(kv.at[odd * helpers + left], recv_x.at[0, odd])
        arrived(kv.at[even * helpers + right], recv_x.at[1, even])
        arrived(kv.at[even * helpers + across], recv_far.at[even])
        arrived(kv.at[odd * helpers + across], recv_far.at[odd])
        return carry

    lax.fori_loop(0, groups // 2, rest, 0)
    for copy in plan:
        copy.wait()

    scale = DH**-0.5 * math.log2(math.e)

    def attend(i, carry):
        source = (z + spread(groups, i)) % groups
        tile = source * helpers + x
        arrived(qs.at[source], recv_q.at[source])
        query = qs[source]
        count = counts[z, tile]
        first = lists[tile, 0]
        chosen = [first] + [
            jnp.where(j < count, lists[tile, j], first) for j in range(1, SLOTS)
        ]
        most = None
        for j in range(0, SLOTS, 2):
            keys = jnp.concatenate((kv[chosen[j], 0], kv[chosen[j + 1], 0]), axis=0)
            part = lax.dot_general(
                query, keys, (((1,), (1,)), ((), ())), preferred_element_type=jnp.float32
            )
            scores[j // 2] = part
            most = part if most is None else jnp.maximum(most, part)
        top = jnp.max(most, axis=1, keepdims=True) * scale
        total = jnp.zeros((TILE, DH), jnp.float32)
        mixed = jnp.zeros((TILE, DH), jnp.float32)
        for j in range(0, SLOTS, 2):
            weights = []
            for k in (j, j + 1):
                shift = top + jnp.where(k < count, 0.0, 1e30).astype(jnp.float32)
                part = scores[j // 2, :, (k - j) * TILE : (k - j + 1) * TILE]
                weight = jnp.exp2(part * scale - shift)
                total += weight
                weights.append(weight.astype(jnp.bfloat16))
            values = jnp.concatenate((kv[chosen[j], 1], kv[chosen[j + 1], 1]), axis=0)
            mixed += lax.dot_general(
                jnp.concatenate(weights, axis=1),
                values,
                (((1,), (0,)), ((), ())),
                preferred_element_type=jnp.float32,
            )
        outs[source] = (mixed / jnp.sum(total, axis=1, keepdims=True)).astype(jnp.bfloat16)

        @pl.when(i == 0)
        def _():
            pltpu.make_async_copy(outs.at[z], landed.at[:, columns(z)], recv_o.at[z]).start()

        @pl.when(i > 0)
        def _():
            pltpu.make_async_remote_copy(
                src_ref=outs.at[source],
                dst_ref=landed.at[:, columns(z)],
                send_sem=send_o,
                recv_sem=recv_o.at[z],
                device_id={"seq": source},
                device_id_type=MESH,
            ).start()

        return carry

    lax.fori_loop(0, groups, attend, 0)

    away = groups - 1
    for which in (0, 1):
        arrived(kv.at[pl.ds(0, away), which], send_kv.at[which])
    arrived(qs.at[pl.ds(0, away)], send_q)
    for which in (0, 1):
        arrived(kv.at[pl.ds(0, groups)], send_x.at[which])
    arrived(kv.at[pl.ds(0, groups)], send_x.at[2])

    def take(i, carry):
        head = (z + spread(groups, i)) % groups
        arrived(landed.at[:, columns(head)], recv_o.at[head])
        return carry

    lax.fori_loop(0, groups, take, 0)
    arrived(outs.at[pl.ds(0, away)], send_o)
    write = pltpu.make_async_copy(landed, out_hbm, write_sem)
    write.start()
    write.wait()


def solution(mesh):
    groups, helpers = mesh.shape["seq"], mesh.shape["help"]
    tiles = groups * helpers
    dma = pltpu.SemaphoreType.DMA

    def shards(query_states, key_states, value_states, tile_lists, tile_counts):
        heads = tile_lists.shape[0]
        return pl.pallas_call(
            functools.partial(kernel, groups, helpers),
            out_shape=jax.ShapeDtypeStruct(query_states.shape, jnp.bfloat16),
            in_specs=[pl.BlockSpec(memory_space=pl.ANY)] * 5,
            out_specs=pl.BlockSpec(memory_space=pl.ANY),
            scratch_shapes=[
                pltpu.VMEM((tiles, 2, TILE, DH), jnp.bfloat16),
                pltpu.VMEM((groups, TILE, DH), jnp.bfloat16),
                pltpu.VMEM((groups, TILE, DH), jnp.bfloat16),
                pltpu.VMEM((SLOTS // 2, TILE, 2 * TILE), jnp.float32),
                pltpu.VMEM((TILE, groups * DH), jnp.bfloat16),
                pltpu.SMEM((tiles, SLOTS), jnp.int32),
                pltpu.SMEM((heads, tiles), jnp.int32),
                dma((2,)),
                dma((1,)),
                dma,
                dma((2,)),
                dma,
                dma((3,)),
                dma((groups,)),
                dma((groups,)),
                dma((groups,)),
                dma((2, groups)),
                dma((groups,)),
                dma,
            ],
            compiler_params=pltpu.CompilerParams(
                collective_id=0, has_side_effects=True, vmem_limit_bytes=24 * 2**20
            ),
            cost_estimate=pl.CostEstimate(
                flops=4 * groups * SLOTS * TILE**3,
                bytes_accessed=4 * TILE * groups * DH * 2,
                transcendentals=groups * SLOTS * TILE**2,
            ),
        )(tile_lists, tile_counts, query_states, key_states, value_states)

    rows = P(("clip", "seq", "help"), None)
    return jax.shard_map(
        shards,
        mesh=mesh,
        in_specs=(rows, rows, rows, P("clip", None, None), P("clip", None)),
        out_specs=rows,
        check_vma=False,
    )
```

time: 610 us -> 119 us (0.20)
  the two profiles are of different devices: /device:TPU:81 before, /device:TPU:56 now
where the time goes in v1:
time: 119 us
  Pallas kernels  115 us (97%)
  local copies, waits for them, and re-layouts  4.04 us (3%)
    pallas_call x1, Pallas kernels, shards(): pl.pallas_call(functools.partial(kernel, groups, helpers), out_shape=jax....  115 us
    unnamed x10, local copies, waits for them, and re-layouts  4.04 us

profile of v1, /device:TPU:56, one launch (start us, length us, event | category | flops | bytes accessed | tf_op | source)
XLA Modules:
  0.0 119.1 jit_solution(780666728408039230)
XLA Ops:
  0.0 0.0 copy-start.3
  0.0 0.0 copy-start
  0.0 1.2 copy.6.lists_hbm
  1.2 0.0 copy-done.3
  1.2 0.0 copy-done
  1.2 0.0 copy-start.1
  1.2 1.0 copy-done.1
  2.2 0.0 copy-start.2
  2.2 1.0 copy-done.2
  3.3 115.0 %shard_map.55 = bf16[128,2048]{1,0:T(8,128)(2,1)S(1)} custom-call(s32[16,64,16]{2,1,0:T(8,128)S(1)} %copy.6.lists_hbm, s32[16,64]{1,0:T(8,128)S(1)} %copy-done.3, bf16[128,2048]{1,0:T(8,128)(2,1)S(1)} %copy-done, bf16[128,2048]{1,0:T(8,128)(2,1)S(1)} %copy-done.1, bf16[128,2048]{1,0:T(8,128)(2,1)S(1)} %copy-done.2), custom_call_target="tpu_custom_call" | custom-call | flops 2147483648 | bytes 2097152 | tf_op jit(solution)/shard_map/pallas_call | solution.py:229
  118.3 0.8 copy.8
Async XLA Ops:
  0.0 1.2 copy-start.3
  0.0 1.2 copy-start
  1.2 1.0 copy-start.1
  2.2 1.0 copy-start.2

commit v2 on v1

--- a/solution.py
+++ b/solution.py
@@ -21,17 +21,26 @@
 
 def kernel(
     groups, helpers,
-    lists_hbm, counts_hbm, q_hbm, k_hbm, v_hbm, out_hbm,
-    kv, qs, outs, scores, landed, lists, counts,
-    plan_sem, own_sem, send_q, send_kv, send_o, send_x,
-    recv_q, recv_kv, recv_o, recv_x, recv_far, write_sem,
+    lists_hbm, counts_hbm, q_hbm, k_hbm, v_hbm, out_ref,
+    kv, qs, outs, scores, lists, counts,
+    plan_sem, up, down, send_q, send_kv, send_o, send_x,
+    recv_q, recv_kv, recv_o, recv_x, recv_far,
 ):
     z = lax.axis_index("seq")
     x = lax.axis_index("help")
     right = (x + 1) % helpers
     left = (x + helpers - 1) % helpers
     across = (x + 2) % helpers
+    above = (z + 1) % groups
+    below = (z + groups - 1) % groups
+    half = groups // 2
     mine = z * helpers + x
+
+    barrier = pltpu.get_barrier_semaphore()
+    for near in (above, below):
+        pl.semaphore_signal(barrier, inc=1, device_id={"seq": near}, device_id_type=MESH)
+    for near in (left, right):
+        pl.semaphore_signal(barrier, inc=1, device_id={"help": near}, device_id_type=MESH)
 
     plan = [
         pltpu.make_async_copy(lists_hbm.at[z], lists, plan_sem.at[0]),
@@ -51,21 +60,7 @@
     for copy in own:
         copy.start()
 
-    barrier = pltpu.get_barrier_semaphore()
-
-    def greet(i, carry):
-        pl.semaphore_signal(
-            barrier, inc=1, device_id={"seq": (z + i) % groups}, device_id_type=MESH
-        )
-        return carry
-
-    lax.fori_loop(1, groups, greet, 0)
-    for near in (left, right):
-        pl.semaphore_signal(barrier, inc=1, device_id={"help": near}, device_id_type=MESH)
-    pl.semaphore_wait(barrier, groups + 1)
-
-    def send_keys(i, carry):
-        there = (z + spread(groups, i)) % groups
+    def send_keys(there):
         for which, source in ((0, k_hbm), (1, v_hbm)):
             pltpu.make_async_remote_copy(
                 src_ref=source.at[:, columns(there)],
@@ -75,10 +70,35 @@
                 device_id={"seq": there},
                 device_id_type=MESH,
             ).start()
-        return carry
+
+    def tell(distance):
+        pl.semaphore_signal(
+            up.at[distance + 1], inc=1, device_id={"seq": above}, device_id_type=MESH
+        )
+        pl.semaphore_signal(
+            down.at[distance + 1], inc=1, device_id={"seq": below}, device_id_type=MESH
+        )
+
+    pl.semaphore_wait(barrier, 4)
+    tell(1)
+    send_keys(above)
+    send_keys(below)
+
+    def wave(distance, carry):
+        pl.semaphore_wait(up.at[distance], 1)
+        pl.semaphore_wait(down.at[distance], 1)
+        tell(distance)
+        send_keys((z + distance) % groups)
+        send_keys((z + groups - distance) % groups)
+        return carry
+
+    lax.fori_loop(2, half, wave, 0)
+    pl.semaphore_wait(up.at[half], 1)
+    pl.semaphore_wait(down.at[half], 1)
+    send_keys((z + half) % groups)
 
     def send_queries(i, carry):
-        there = (z + spread(groups, i)) % groups
+        there = (z + spread(groups, groups - 1 - i)) % groups
         pltpu.make_async_remote_copy(
             src_ref=q_hbm.at[:, columns(there)],
             dst_ref=qs.at[z],
@@ -89,10 +109,9 @@
         ).start()
         return carry
 
-    lax.fori_loop(1, groups, send_keys, 0)
-    lax.fori_loop(1, groups, send_queries, 0)
-
-    def tile_copy(tile, way, sem, send, near):
+    lax.fori_loop(0, groups - 1, send_queries, 0)
+
+    def tile_copy(tile, sem, send, near):
         return pltpu.make_async_remote_copy(
             src_ref=kv.at[tile],
             dst_ref=kv.at[tile],
@@ -109,23 +128,30 @@
         source = (z + spread(groups, i)) % groups
         tile = source * helpers + x
         arrived(kv.at[tile], recv_kv.at[source])
-        tile_copy(tile, 0, recv_x.at[0, source], 0, right).start()
-        tile_copy(tile, 1, recv_x.at[1, source], 1, left).start()
-        return carry
-
-    def pass_far(i, carry):
+        tile_copy(tile, recv_x.at[0, source], 0, right).start()
+        tile_copy(tile, recv_x.at[1, source], 1, left).start()
+        return carry
+
+    def pass_far(i):
         even = (z + spread(groups, i)) % groups
         odd = (z + spread(groups, i + 1)) % groups
         from_left = even * helpers + left
         from_right = odd * helpers + right
         arrived(kv.at[from_left], recv_x.at[0, even])
-        tile_copy(from_left, 0, recv_far.at[even], 2, right).start()
+        tile_copy(from_left, recv_far.at[even], 2, right).start()
         arrived(kv.at[from_right], recv_x.at[1, odd])
-        tile_copy(from_right, 1, recv_far.at[odd], 2, left).start()
-        return carry
-
-    lax.fori_loop(0, groups, pass_on, 0)
-    lax.fori_loop(0, groups // 2, lambda i, c: pass_far(2 * i, c), 0)
+        tile_copy(from_right, recv_far.at[odd], 2, left).start()
+
+    def pass_both(i, carry):
+        pass_on(2 * i, 0)
+        pass_on(2 * i + 1, 0)
+        pass_far(2 * i - 2)
+        return carry
+
+    pass_on(0, 0)
+    pass_on(1, 0)
+    lax.fori_loop(1, half, pass_both, 0)
+    pass_far(groups - 2)
 
     def rest(i, carry):
         even = (z + spread(groups, 2 * i)) % groups
@@ -136,21 +162,21 @@
         arrived(kv.at[odd * helpers + across], recv_far.at[odd])
         return carry
 
-    lax.fori_loop(0, groups // 2, rest, 0)
+    lax.fori_loop(0, half, rest, 0)
     for copy in plan:
         copy.wait()
 
     scale = DH**-0.5 * math.log2(math.e)
 
     def attend(i, carry):
-        source = (z + spread(groups, i)) % groups
+        source = (z + spread(groups, groups - 1 - i)) % groups
         tile = source * helpers + x
         arrived(qs.at[source], recv_q.at[source])
         query = qs[source]
         count = counts[z, tile]
-        first = lists[tile, 0]
+        first = lists[0, tile]
         chosen = [first] + [
-            jnp.where(j < count, lists[tile, j], first) for j in range(1, SLOTS)
+            jnp.where(j < count, lists[j, tile], first) for j in range(1, SLOTS)
         ]
         most = None
         for j in range(0, SLOTS, 2):
@@ -180,15 +206,15 @@
             )
         outs[source] = (mixed / jnp.sum(total, axis=1, keepdims=True)).astype(jnp.bfloat16)
 
-        @pl.when(i == 0)
+        @pl.when(i == groups - 1)
         def _():
-            pltpu.make_async_copy(outs.at[z], landed.at[:, columns(z)], recv_o.at[z]).start()
-
-        @pl.when(i > 0)
+            pltpu.make_async_copy(outs.at[z], out_ref.at[:, columns(z)], recv_o.at[z]).start()
+
+        @pl.when(i < groups - 1)
         def _():
             pltpu.make_async_remote_copy(
                 src_ref=outs.at[source],
-                dst_ref=landed.at[:, columns(z)],
+                dst_ref=out_ref.at[:, columns(z)],
                 send_sem=send_o,
                 recv_sem=recv_o.at[z],
                 device_id={"seq": source},
@@ -203,20 +229,15 @@
     for which in (0, 1):
         arrived(kv.at[pl.ds(0, away), which], send_kv.at[which])
     arrived(qs.at[pl.ds(0, away)], send_q)
-    for which in (0, 1):
+    for which in (0, 1, 2):
         arrived(kv.at[pl.ds(0, groups)], send_x.at[which])
-    arrived(kv.at[pl.ds(0, groups)], send_x.at[2])
 
     def take(i, carry):
-        head = (z + spread(groups, i)) % groups
-        arrived(landed.at[:, columns(head)], recv_o.at[head])
+        arrived(out_ref.at[:, columns(i)], recv_o.at[i])
         return carry
 
     lax.fori_loop(0, groups, take, 0)
     arrived(outs.at[pl.ds(0, away)], send_o)
-    write = pltpu.make_async_copy(landed, out_hbm, write_sem)
-    write.start()
-    write.wait()
 
 
 def solution(mesh):
@@ -236,11 +257,11 @@
                 pltpu.VMEM((groups, TILE, DH), jnp.bfloat16),
                 pltpu.VMEM((groups, TILE, DH), jnp.bfloat16),
                 pltpu.VMEM((SLOTS // 2, TILE, 2 * TILE), jnp.float32),
-                pltpu.VMEM((TILE, groups * DH), jnp.bfloat16),
-                pltpu.SMEM((tiles, SLOTS), jnp.int32),
+                pltpu.SMEM((SLOTS, tiles), jnp.int32),
                 pltpu.SMEM((heads, tiles), jnp.int32),
                 dma((2,)),
-                dma((1,)),
+                pltpu.SemaphoreType.REGULAR((groups // 2 + 1,)),
+                pltpu.SemaphoreType.REGULAR((groups // 2 + 1,)),
                 dma,
                 dma((2,)),
                 dma,
@@ -250,17 +271,16 @@
                 dma((groups,)),
                 dma((2, groups)),
                 dma((groups,)),
-                dma,
             ],
             compiler_params=pltpu.CompilerParams(
-                collective_id=0, has_side_effects=True, vmem_limit_bytes=24 * 2**20
+                collective_id=0, has_side_effects=True, vmem_limit_bytes=60 * 2**20
             ),
             cost_estimate=pl.CostEstimate(
                 flops=4 * groups * SLOTS * TILE**3,
                 bytes_accessed=4 * TILE * groups * DH * 2,
                 transcendentals=groups * SLOTS * TILE**2,
             ),
-        )(tile_lists, tile_counts, query_states, key_states, value_states)
+        )(jnp.swapaxes(tile_lists, 1, 2), tile_counts, query_states, key_states, value_states)
 
     rows = P(("clip", "seq", "help"), None)
     return jax.shard_map(

time: 119 us -> 114 us (0.958)
  Pallas kernels: 115 us -> 112 us
  local copies, waits for them, and re-layouts: 4.04 us -> 1.88 us
    pallas_call x1, Pallas kernels: 115 us -> 112 us  [shards(): pl.pallas_call(functools.partial(kernel, groups, helpers), out_shape=jax....]
    unnamed x10 -> x1, local copies, waits for them, and re-layouts: 4.04 us -> 1.88 us
where the time goes in v2:
time: 114 us
  Pallas kernels  112 us (98%)
  local copies, waits for them, and re-layouts  1.88 us (2%)
    pallas_call x1, Pallas kernels, shards(): pl.pallas_call(functools.partial(kernel, groups, helpers), out_shape=jax....  112 us

profile of v2, /device:TPU:56, one launch (start us, length us, event | category | flops | bytes accessed | tf_op | source)
XLA Modules:
  0.0 113.5 jit_solution(7779288313202187011)
XLA Ops:
  0.0 111.6 %shard_map.55 = bf16[128,2048]{1,0:T(8,128)(2,1)} custom-call(s32[16,16,64]{2,1,0:T(8,128)} %bitcast.1, s32[16,64]{1,0:T(8,128)} %counts_hbm.1, bf16[128,2048]{1,0:T(8,128)(2,1)} %q_hbm.1, bf16[128,2048]{1,0:T(8,128)(2,1)} %k_hbm.1, bf16[128,2048]{1,0:T(8,128)(2,1)} %v_hbm.1), custom_call_target="tpu_custom_call" | custom-call | flops 2147483648 | bytes 2097152 | tf_op jit(solution)/shard_map/pallas_call | solution.py:250
  111.6 1.9 %copy.7 = bf16[128,2048]{1,0:T(8,128)(2,1)} copy(bf16[128,2048]{1,0:T(8,128)(2,1)} %shard_map.55) | data formatting | bytes 1048576

commit v3 on v2

--- a/solution.py
+++ b/solution.py
@@ -98,7 +98,7 @@
     send_keys((z + half) % groups)
 
     def send_queries(i, carry):
-        there = (z + spread(groups, groups - 1 - i)) % groups
+        there = (z + spread(groups, i + 1)) % groups
         pltpu.make_async_remote_copy(
             src_ref=q_hbm.at[:, columns(there)],
             dst_ref=qs.at[z],
@@ -169,7 +169,7 @@
     scale = DH**-0.5 * math.log2(math.e)
 
     def attend(i, carry):
-        source = (z + spread(groups, groups - 1 - i)) % groups
+        source = (i // 4) * 4 + (z + i) % 4
         tile = source * helpers + x
         arrived(qs.at[source], recv_q.at[source])
         query = qs[source]
@@ -206,11 +206,11 @@
             )
         outs[source] = (mixed / jnp.sum(total, axis=1, keepdims=True)).astype(jnp.bfloat16)
 
-        @pl.when(i == groups - 1)
+        @pl.when(source == z)
         def _():
             pltpu.make_async_copy(outs.at[z], out_ref.at[:, columns(z)], recv_o.at[z]).start()
 
-        @pl.when(i < groups - 1)
+        @pl.when(source != z)
         def _():
             pltpu.make_async_remote_copy(
                 src_ref=outs.at[source],
@@ -249,7 +249,7 @@
         heads = tile_lists.shape[0]
         return pl.pallas_call(
             functools.partial(kernel, groups, helpers),
-            out_shape=jax.ShapeDtypeStruct(query_states.shape, jnp.bfloat16),
+            out_shape=pltpu.VMEM(query_states.shape, jnp.bfloat16),
             in_specs=[pl.BlockSpec(memory_space=pl.ANY)] * 5,
             out_specs=pl.BlockSpec(memory_space=pl.ANY),
             scratch_shapes=[
@@ -273,7 +273,7 @@
                 dma((groups,)),
             ],
             compiler_params=pltpu.CompilerParams(
-                collective_id=0, has_side_effects=True, vmem_limit_bytes=60 * 2**20
+                collective_id=0, has_side_effects=True, vmem_limit_bytes=62 * 2**20
             ),
             cost_estimate=pl.CostEstimate(
                 flops=4 * groups * SLOTS * TILE**3,

time: 114 us -> 110 us (0.965)
  Pallas kernels: 112 us -> 109 us
    pallas_call x1, Pallas kernels: 112 us -> 109 us  [shards(): pl.pallas_call(functools.partial(kernel, groups, helpers), out_shape=pltp...]
where the time goes in v3:
time: 110 us
  Pallas kernels  109 us (99%)
    pallas_call x1, Pallas kernels, shards(): pl.pallas_call(functools.partial(kernel, groups, helpers), out_shape=pltp...  109 us

profile of v3, /device:TPU:56, one launch (start us, length us, event | category | flops | bytes accessed | tf_op | source)
XLA Modules:
  0.0 110.3 jit_solution(12897799140796427941)
XLA Ops:
  0.0 109.5 %shard_map.55 = bf16[128,2048]{1,0:T(8,128)(2,1)S(1)} custom-call(s32[16,16,64]{2,1,0:T(8,128)} %bitcast.1, s32[16,64]{1,0:T(8,128)} %counts_hbm.1, bf16[128,2048]{1,0:T(8,128)(2,1)} %q_hbm.1, bf16[128,2048]{1,0:T(8,128)(2,1)} %k_hbm.1, bf16[128,2048]{1,0:T(8,128)(2,1)} %v_hbm.1), custom_call_target="tpu_custom_call" | custom-call | flops 2147483648 | bytes 2097152 | tf_op jit(solution)/shard_map/pallas_call | solution.py:250
  109.5 0.8 copy.7

commit v4 on v3

--- a/solution.py
+++ b/solution.py
@@ -97,19 +97,26 @@
     pl.semaphore_wait(down.at[half], 1)
     send_keys((z + half) % groups)
 
+    def turn(i):
+        return (i // 4) * 4 + (z + i) % 4
+
     def send_queries(i, carry):
-        there = (z + spread(groups, i + 1)) % groups
-        pltpu.make_async_remote_copy(
-            src_ref=q_hbm.at[:, columns(there)],
-            dst_ref=qs.at[z],
-            send_sem=send_q,
-            recv_sem=recv_q.at[z],
-            device_id={"seq": there},
-            device_id_type=MESH,
-        ).start()
-        return carry
-
-    lax.fori_loop(0, groups - 1, send_queries, 0)
+        there = turn(i)
+
+        @pl.when(there != z)
+        def _():
+            pltpu.make_async_remote_copy(
+                src_ref=q_hbm.at[:, columns(there)],
+                dst_ref=qs.at[z],
+                send_sem=send_q,
+                recv_sem=recv_q.at[z],
+                device_id={"seq": there},
+                device_id_type=MESH,
+            ).start()
+
+        return carry
+
+    lax.fori_loop(0, groups, send_queries, 0)
 
     def tile_copy(tile, sem, send, near):
         return pltpu.make_async_remote_copy(
@@ -169,7 +176,7 @@
     scale = DH**-0.5 * math.log2(math.e)
 
     def attend(i, carry):
-        source = (i // 4) * 4 + (z + i) % 4
+        source = turn(i)
         tile = source * helpers + x
         arrived(qs.at[source], recv_q.at[source])
         query = qs[source]

time: 110 us -> 110 us (level)
  no operation moved by 1% of the time
where the time goes in v4:
time: 110 us; the launch traced here: 109 us
  Pallas kernels  108 us (98%)
    pallas_call x1, Pallas kernels, shards(): pl.pallas_call(functools.partial(kernel, groups, helpers), out_shape=pltp...  108 us

profile of v4, /device:TPU:56, one launch (start us, length us, event | category | flops | bytes accessed | tf_op | source)
XLA Modules:
  0.0 109.3 jit_solution(16073381632479041102)
XLA Ops:
  0.0 108.5 %shard_map.55 = bf16[128,2048]{1,0:T(8,128)(2,1)S(1)} custom-call(s32[16,16,64]{2,1,0:T(8,128)} %bitcast.1, s32[16,64]{1,0:T(8,128)} %counts_hbm.1, bf16[128,2048]{1,0:T(8,128)(2,1)} %q_hbm.1, bf16[128,2048]{1,0:T(8,128)(2,1)} %k_hbm.1, bf16[128,2048]{1,0:T(8,128)(2,1)} %v_hbm.1), custom_call_target="tpu_custom_call" | custom-call | flops 2147483648 | bytes 2097152 | tf_op jit(solution)/shard_map/pallas_call | solution.py:257
  108.5 0.8 copy.7

commit v5 on v4

--- a/solution.py
+++ b/solution.py
@@ -175,10 +175,8 @@
 
     scale = DH**-0.5 * math.log2(math.e)
 
-    def attend(i, carry):
-        source = turn(i)
+    def prepare(source, buffer):
         tile = source * helpers + x
-        arrived(qs.at[source], recv_q.at[source])
         query = qs[source]
         count = counts[z, tile]
         first = lists[0, tile]
@@ -191,16 +189,18 @@
             part = lax.dot_general(
                 query, keys, (((1,), (1,)), ((), ())), preferred_element_type=jnp.float32
             )
-            scores[j // 2] = part
+            scores[buffer, j // 2] = part
             most = part if most is None else jnp.maximum(most, part)
-        top = jnp.max(most, axis=1, keepdims=True) * scale
+        return jnp.max(most, axis=1, keepdims=True) * scale, count, chosen
+
+    def mix(source, buffer, top, count, chosen):
         total = jnp.zeros((TILE, DH), jnp.float32)
         mixed = jnp.zeros((TILE, DH), jnp.float32)
         for j in range(0, SLOTS, 2):
             weights = []
             for k in (j, j + 1):
                 shift = top + jnp.where(k < count, 0.0, 1e30).astype(jnp.float32)
-                part = scores[j // 2, :, (k - j) * TILE : (k - j + 1) * TILE]
+                part = scores[buffer, j // 2, :, (k - j) * TILE : (k - j + 1) * TILE]
                 weight = jnp.exp2(part * scale - shift)
                 total += weight
                 weights.append(weight.astype(jnp.bfloat16))
@@ -213,6 +213,7 @@
             )
         outs[source] = (mixed / jnp.sum(total, axis=1, keepdims=True)).astype(jnp.bfloat16)
 
+    def send_back(source):
         @pl.when(source == z)
         def _():
             pltpu.make_async_copy(outs.at[z], out_ref.at[:, columns(z)], recv_o.at[z]).start()
@@ -228,9 +229,18 @@
                 device_id_type=MESH,
             ).start()
 
-        return carry
-
-    lax.fori_loop(0, groups, attend, 0)
+    def attend(i, carry):
+        one, two = turn(2 * i), turn(2 * i + 1)
+        arrived(qs.at[one], recv_q.at[one])
+        arrived(qs.at[two], recv_q.at[two])
+        first, second = prepare(one, 0), prepare(two, 1)
+        mix(one, 0, *first)
+        mix(two, 1, *second)
+        send_back(one)
+        send_back(two)
+        return carry
+
+    lax.fori_loop(0, half, attend, 0)
 
     away = groups - 1
     for which in (0, 1):
@@ -263,7 +273,7 @@
                 pltpu.VMEM((tiles, 2, TILE, DH), jnp.bfloat16),
                 pltpu.VMEM((groups, TILE, DH), jnp.bfloat16),
                 pltpu.VMEM((groups, TILE, DH), jnp.bfloat16),
-                pltpu.VMEM((SLOTS // 2, TILE, 2 * TILE), jnp.float32),
+                pltpu.VMEM((2, SLOTS // 2, TILE, 2 * TILE), jnp.float32),
                 pltpu.SMEM((SLOTS, tiles), jnp.int32),
                 pltpu.SMEM((heads, tiles), jnp.int32),
                 dma((2,)),

time: 110 us -> 110 us (level)
  no operation moved by 1% of the time
where the time goes in v5:
time: 110 us; the launch traced here: 109 us
  Pallas kernels  108 us (98%)
    pallas_call x1, Pallas kernels, shards(): pl.pallas_call(functools.partial(kernel, groups, helpers), out_shape=pltp...  108 us

profile of v5, /device:TPU:56, one launch (start us, length us, event | category | flops | bytes accessed | tf_op | source)
XLA Modules:
  0.0 109.1 jit_solution(8999242462668989720)
XLA Ops:
  0.0 108.3 %shard_map.55 = bf16[128,2048]{1,0:T(8,128)(2,1)S(1)} custom-call(s32[16,16,64]{2,1,0:T(8,128)} %bitcast.1, s32[16,64]{1,0:T(8,128)} %counts_hbm.1, bf16[128,2048]{1,0:T(8,128)(2,1)} %q_hbm.1, bf16[128,2048]{1,0:T(8,128)(2,1)} %k_hbm.1, bf16[128,2048]{1,0:T(8,128)(2,1)} %v_hbm.1), custom_call_target="tpu_custom_call" | custom-call | flops 2147483648 | bytes 2097152 | tf_op jit(solution)/shard_map/pallas_call | solution.py:267
  108.3 0.8 copy.7
